TPU v7x, 256 devices: a whole 4x4x8 slice. The times are simulated.
256 devices in a mesh: samp: 16 (over z, y_lo), par: 16 (over y_hi, x, core).
Axes of the slice: x: 4, y: 4 (y_hi: 2, y_lo: 2; y = y_hi * 2 + y_lo), z: 8, core: 2. Of those that a mesh axis runs over, the one named last changes fastest.
Arguments:
- jacobian: bfloat16 [16384, 8192], P('samp', 'par')
- partners: int32 [2, 16], replicated, may hold values from 0 to 15, as said below
Outputs:
- diag_tiles: float32 [16384, 1024], P(('samp', 'par'))
- cross_tiles: float32 [2, 16384, 1024], P(None, ('samp', 'par'))
Inputs may be any that keep to these rules, and one draw needn't show every extreme that they name: partners[r, i] = i XOR m_r with a mask m_r taken from the seed; m_0 is neither 0 nor 16 - 1, and m_1 = m_0 XOR (15).
All inputs are finite; a program needn't handle non-finite values.
Results may differ from a plain program's by a relative error of at most 0.004.
Values may be sent and summed in bfloat16 or wider, within the bound.
No kernel may reach another device: no remote copies, remote signals or barrier semaphores. Data moves between devices by JAX's collectives and lax.ppermute only.
A program may use at most 64 MiB of HBM per device.

v0:
```python
import functools

import jax
import jax.numpy as jnp
from jax import lax
from jax.experimental import pallas as pl
from jax.experimental.pallas import tpu as pltpu
from jax.sharding import Mesh, PartitionSpec as P

SAMP = ("z", "y_lo")
PAR = ("y_hi", "x", "core")
CHIPS = ("y_hi", "x")
BITS = {1: (0, 1), 2: (1, 3), 3: (1, 3), 4: (2, 1), 5: (2, 1), 6: (1, 3), 7: (2, 3)}
TILE = 256


def parity(block, mask):
    s, t = BITS[mask]
    return ((block >> s) ^ (block >> t)) & 1


def sources(mask):
    return [i ^ (mask ^ 15 if parity(i, mask) else mask) for i in range(16)]


def gram(a, b):
    return lax.dot_general(a, b, (((1,), (1,)), ((), ())), preferred_element_type=jnp.float32)


def centre(x, mean):
    return (x.astype(jnp.float32) - mean).astype(jnp.bfloat16)


def vmem_call(kernel, outs, scratch, flops):
    return pl.pallas_call(
        kernel,
        out_shape=outs,
        scratch_shapes=scratch,
        cost_estimate=pl.CostEstimate(flops=flops, bytes_accessed=6 << 20, transcendentals=0),
        compiler_params=pltpu.CompilerParams(vmem_limit_bytes=24 << 20),
    )


def add_totals(ref, side, total_ref):
    ones = jnp.ones((16, 1024), jnp.bfloat16)
    total = jnp.dot(ones, ref[...], preferred_element_type=jnp.float32)
    for r in range(4):
        total_ref[:, side * 4 + r, :] = total[:, r * 128 : (r + 1) * 128]


def own_total_kernel(own_ref, partners_ref, total_ref, index_ref):
    first = partners_ref[0, 0]
    index_ref[0] = jnp.minimum(first, 15 - first) - 1
    total_ref[...] = jnp.zeros_like(total_ref)
    add_totals(own_ref, 0, total_ref)


def sister_total_kernel(sister_ref, before_ref, total_ref):
    total_ref[...] = before_ref[...]
    add_totals(sister_ref, 1, total_ref)


def half_kernel(own_ref, sister_ref, core_ref, half_ref):
    core = core_ref[0]

    @pl.loop(0, 8)
    def _(c):
        at = pl.ds(pl.multiple_of(c * 64, 64), 64)
        half = pl.ds(pl.multiple_of(c * 128 + core * 64, 64), 64)
        half_ref[at, :512] = own_ref[half, :]
        half_ref[at, 512:] = sister_ref[half, :]


def column_mean(totals_ref):
    mean = jnp.sum(totals_ref[...], axis=0) * (1.0 / 16384)
    return jnp.concatenate([mean[r : r + 1] for r in range(8)], axis=1)


def own_kernel(own_ref, sister_ref, totals_ref, core_ref, centred_ref, out_ref, rows):
    mean = column_mean(totals_ref)
    core = core_ref[0]

    @pl.loop(0, 8)
    def _(c):
        at = pl.ds(pl.multiple_of(c * 128, 128), 128)
        centred_ref[at, :512] = centre(own_ref[at, :], mean[:, :512])
        centred_ref[at, 512:] = centre(sister_ref[at, :], mean[:, 512:])
        half = pl.ds(pl.multiple_of(c * 128 + core * 64, 64), 64)
        put = pl.ds(pl.multiple_of(((c & 3) * 2 + (c >> 2)) * 64, 64), 64)
        rows[put, :] = centred_ref[half, :]

    @pl.loop(0, 1024 // TILE)
    def _(n):
        at = pl.ds(pl.multiple_of(n * TILE, TILE), TILE)
        out_ref[:, at] = gram(rows[...], centred_ref[at, :]).astype(jnp.bfloat16)


def cross_kernel(raw_ref, totals_ref, centred_ref, out_ref, raw, rows, out, in_sem, out_sem):
    arrive = pltpu.make_async_copy(raw_ref, raw, in_sem)
    arrive.start()
    mean = column_mean(totals_ref)
    arrive.wait()
    rows[...] = centre(raw[...], mean)
    leave = []
    for n in range(1024 // TILE):
        at = pl.ds(n * TILE, TILE)
        out[:, at] = gram(rows[...], centred_ref[at, :]).astype(jnp.bfloat16)
        leave.append(pltpu.make_async_copy(out.at[:, at], out_ref.at[:, at], out_sem.at[n]))
        leave[-1].start()
    for copy in leave:
        copy.wait()


def fold_kernel(got_ref, result_ref, tiles_ref):
    total = jnp.sum(got_ref[...].astype(jnp.float32), axis=0)
    result_ref[...] = total.astype(jnp.bfloat16)
    for b in range(8):
        turned = total[:, b * 128 : (b + 1) * 128].T
        for p in range(2):
            tile = turned[p * 64 : (p + 1) * 64]
            tiles_ref[2 * b + p] = jnp.concatenate([tile[:32], tile[32:]], axis=1).astype(jnp.bfloat16)


def output_kernel(arrived_ref, tiles_ref, keep_ref, other_ref, place_ref, diag_ref, out_ref):
    place = place_ref[0]
    diag_ref[...] = keep_ref[...] + other_ref[...].astype(jnp.float32)
    out_ref[1 - place] = arrived_ref[...].astype(jnp.float32)
    for q in range(16):
        tile = tiles_ref[q].astype(jnp.float32)
        out_ref[place, :32, q * 64 : (q + 1) * 64] = tile[:, :64]
        out_ref[place, 32:, q * 64 : (q + 1) * 64] = tile[:, 64:]


def exchange(mask, total, jac, sister, core):
    totals = lax.all_to_all(total, SAMP, 0, 0, tiled=True)
    half = pl.pallas_call(
        half_kernel,
        out_shape=jax.ShapeDtypeStruct((512, 1024), jnp.bfloat16),
        in_specs=[pl.BlockSpec(memory_space=pltpu.VMEM)] * 2 + [pl.BlockSpec(memory_space=pltpu.SMEM)],
        cost_estimate=pl.CostEstimate(flops=0, bytes_accessed=2 << 20, transcendentals=0),
        compiler_params=pltpu.CompilerParams(vmem_limit_bytes=24 << 20),
    )(jac, sister, core)
    raw = lax.ppermute(half, SAMP, [(s, d) for d, s in enumerate(sources(mask))])
    own, partial = pl.pallas_call(
        own_kernel,
        out_shape=(
            jax.ShapeDtypeStruct((1024, 1024), jnp.bfloat16),
            jax.ShapeDtypeStruct((512, 1024), jnp.bfloat16),
        ),
        in_specs=[pl.BlockSpec(memory_space=pltpu.VMEM)] * 3 + [pl.BlockSpec(memory_space=pltpu.SMEM)],
        scratch_shapes=[pltpu.VMEM((512, 1024), jnp.bfloat16)],
        cost_estimate=pl.CostEstimate(flops=2 << 31, bytes_accessed=6 << 20, transcendentals=0),
        compiler_params=pltpu.CompilerParams(vmem_limit_bytes=24 << 20),
    )(jac, sister, totals, core)
    diag = lax.all_to_all(partial.reshape(4, 128, 1024), "x", 0, 0, tiled=True)
    return raw, own, diag, totals


def finish(mask, result, tiles):
    back = [(d, s) for d, s in enumerate(sources(mask))]
    arrived = lax.ppermute(result, SAMP, back)
    turned = lax.all_to_all(tiles, PAR, 0, 0, tiled=True)
    return arrived, turned, parity(lax.axis_index(SAMP), mask)


def shards(jac, partners):
    first = partners[0, 0]
    core = lax.axis_index("core")
    sister = lax.ppermute(jac, "core", [(0, 1), (1, 0)])
    sums = jax.ShapeDtypeStruct((16, 8, 128), jnp.float32)
    total, index = pl.pallas_call(
        own_total_kernel,
        out_shape=(sums, jax.ShapeDtypeStruct((1,), jnp.int32)),
        in_specs=[pl.BlockSpec(memory_space=pltpu.VMEM), pl.BlockSpec(memory_space=pltpu.SMEM)],
        out_specs=(pl.BlockSpec(memory_space=pltpu.VMEM), pl.BlockSpec(memory_space=pltpu.SMEM)),
        cost_estimate=pl.CostEstimate(flops=16 << 20, bytes_accessed=1 << 20, transcendentals=0),
        compiler_params=pltpu.CompilerParams(vmem_limit_bytes=24 << 20),
    )(jac, partners)
    index = index[0]
    total = vmem_call(sister_total_kernel, sums, [], 16 << 20)(sister, total)
    raw, own, diag, totals = lax.switch(
        index,
        [functools.partial(exchange, m) for m in range(1, 8)],
        total, jac, sister, core.reshape(1),
    )
    diag = lax.optimization_barrier(diag)
    partial = pl.pallas_call(
        cross_kernel,
        out_shape=jax.ShapeDtypeStruct((512, 1024), jnp.bfloat16),
        in_specs=[pl.BlockSpec(memory_space=pl.ANY)] + [pl.BlockSpec(memory_space=pltpu.VMEM)] * 2,
        out_specs=pl.BlockSpec(memory_space=pl.ANY),
        scratch_shapes=[pltpu.VMEM((512, 1024), jnp.bfloat16)] * 3
        + [pltpu.SemaphoreType.DMA, pltpu.SemaphoreType.DMA((1024 // TILE,))],
        cost_estimate=pl.CostEstimate(flops=2 << 29, bytes_accessed=4 << 20, transcendentals=0),
        compiler_params=pltpu.CompilerParams(vmem_limit_bytes=24 << 20),
    )(raw, totals, own)
    diag = jnp.sum(diag.reshape(4, 2, 64, 1024).astype(jnp.float32), axis=0)
    y_hi = lax.axis_index("y_hi")
    keep, give = jnp.where(y_hi == 0, diag[0], diag[1]), jnp.where(y_hi == 0, diag[1], diag[0])
    other_half = lax.ppermute(give.astype(jnp.bfloat16), "y_hi", [(0, 1), (1, 0)])
    got = lax.all_to_all(partial.reshape(8, 64, 1024), CHIPS, 0, 0, tiled=True)
    result, tiles = vmem_call(
        fold_kernel,
        (
            jax.ShapeDtypeStruct((64, 1024), jnp.bfloat16),
            jax.ShapeDtypeStruct((16, 32, 128), jnp.bfloat16),
        ),
        [],
        1 << 20,
    )(got)
    arrived, turned, par = lax.switch(
        index, [functools.partial(finish, m) for m in range(1, 8)], result, tiles
    )
    place = par ^ (first > 7).astype(jnp.int32)
    return pl.pallas_call(
        output_kernel,
        out_shape=(
            jax.ShapeDtypeStruct((64, 1024), jnp.float32),
            jax.ShapeDtypeStruct((2, 64, 1024), jnp.float32),
        ),
        in_specs=[pl.BlockSpec(memory_space=pltpu.VMEM)] * 4 + [pl.BlockSpec(memory_space=pltpu.SMEM)],
        compiler_params=pltpu.CompilerParams(vmem_limit_bytes=24 << 20),
    )(arrived, turned, keep, other_half, place.reshape(1))


def solution(mesh):
    fine = Mesh(mesh.devices.reshape(8, 2, 2, 4, 2), SAMP + PAR)
    return jax.shard_map(
        shards,
        mesh=fine,
        in_specs=(P(SAMP, PAR), P()),
        out_specs=(P(SAMP + PAR, None), P(None, SAMP + PAR, None)),
        check_vma=False,
    )
```

profile of v0, /device:TPU:33, one launch (start us, length us, event | category | flops | bytes accessed | tf_op | source)
XLA Modules:
  0.0 110.4 jit_solution(8668555438075369175)
XLA Ops:
  0.6 0.8 collective-permute-start.14
  1.4 0.0 copy-start
  1.4 0.7 copy-done
  2.1 0.0 copy-start.2
  2.1 1.9 %shard_map.41 = (f32[16,8,128]{2,1,0:T(8,128)S(1)}, s32[1]{0:T(128)}) custom-call(bf16[1024,512]{1,0:T(8,128)(2,1)} %own_ref.1, s32[2,16]{1,0:T(2,128)S(1)} %copy-done), custom_call_target="tpu_custom_call" | custom-call | flops 16777216 | bytes 1048576 | tf_op jit(solution)/shard_map/pallas_call | solution.py:171
  4.6 0.0 collective-permute-done.14.sister_ref
  4.6 0.9 shard_map.42
  5.5 0.0 copy-done.2
  5.5 61.4 %conditional.2 = (bf16[512,1024]{1,0:T(8,128)(2,1)}, bf16[1024,1024]{1,0:T(8,128)(2,1)S(1)}, bf16[4,128,1024]{2,1,0:T(8,128)(2,1)}, f32[16,8,128]{2,1,0:T(8,128)}) conditional(s32[]{:T(128)} %bitcast.7, (bf16[1024,512]{1,0:T(8,128)(2,1)S(1)}, bf16[1024,512]{1,0:T(8,128)(2,1)S(1)}, s32[1]{0:T(128)}, ...), branch_computations={%region_0.0_spmd, %region_1.0_spmd, %region_2.0_spmd, %region_3.0_... | conditional | flops 4294967296 | bytes 15138948 | solution.py:181
  5.5 9.0 %all-to-all-start.10 = ((f32[16,8,128]{2,1,0:T(8,128)}), f32[16,8,128]{2,1,0:T(8,128)S(1)}, u32[]{:S(2)}, u32[]{:S(2)}) async-start(f32[16,8,128]{2,1,0:T(8,128)} %get-tuple-element.117), calls=%async_computation.10 | async-start | bytes 131072 | tf_op jit(solution)/shard_map/cond/branch_5_fun/all_to_all | solution.py:135
  14.5 0.1 branch_5_fun.2
  14.6 1.3 %collective-permute-start.5 = (bf16[512,1024]{1,0:T(8,128)(2,1)S(1)}, bf16[512,1024]{1,0:T(8,128)(2,1)}, u32[]{:S(2)}, u32[]{:S(2)}) collective-permute-start(bf16[512,1024]{1,0:T(8,128)(2,1)S(1)} %branch_5_fun.2), channel_id=1, source_target_pairs={{96,0},{112,16},{176,32},{160,48},{32,64},{48,80},{240,96},{224,11... | collective-permute-start | bytes 3145736 | tf_op jit(solution)/shard_map/cond/branch_5_fun/ppermute | solution.py:143
  15.9 5.5 %all-to-all-done.10.totals_ref = f32[16,8,128]{2,1,0:T(8,128)S(1)} async-done(((f32[16,8,128]{2,1,0:T(8,128)}), f32[16,8,128]{2,1,0:T(8,128)S(1)}, u32[]{:S(2)}, u32[]{:S(2)}) %all-to-all-start.10) | async-done | bytes 65568 | tf_op jit(solution)/shard_map/cond/branch_5_fun/all_to_all | solution.py:135
  21.4 0.0 copy-start.8
  21.4 2.5 %branch_5_fun.3 = (bf16[1024,1024]{1,0:T(8,128)(2,1)S(1)}, bf16[512,1024]{1,0:T(8,128)(2,1)S(1)}) custom-call(bf16[1024,512]{1,0:T(8,128)(2,1)S(1)} %get-tuple-element.114.own_ref, bf16[1024,512]{1,0:T(8,128)(2,1)S(1)} %get-tuple-element.115.sister_ref, f32[16,8,128]{2,1,0:T(8,128)S(1)} %all-to-all-done.10.totals_ref, s32[1]{0:T(128)} %get-tuple-element.116.core_ref), custom_call_target="tpu_custom_call" | custom-call | flops 4294967296 | bytes 6291456 | tf_op jit(solution)/shard_map/cond/branch_5_fun/pallas_call | solution.py:144
  23.9 0.0 copy-done.8
  23.9 17.3 %all_to_all.94 = bf16[4,128,1024]{2,1,0:T(8,128)(2,1)} all-to-all(bf16[4,128,1024]{2,1,0:T(8,128)(2,1)S(1)} %bitcast.17), channel_id=1, replica_groups=mesh['z'=8,'y_lo'=2,'y_hi'=2,'x'=4,'core'=2] {'x'}, dimensions={0} | all-to-all | bytes 2097152 | tf_op jit(solution)/shard_map/cond/branch_5_fun/all_to_all | solution.py:155
  41.2 25.7 %collective-permute-done.5 = bf16[512,1024]{1,0:T(8,128)(2,1)} collective-permute-done((bf16[512,1024]{1,0:T(8,128)(2,1)S(1)}, bf16[512,1024]{1,0:T(8,128)(2,1)}, u32[]{:S(2)}, u32[]{:S(2)}) %collective-permute-start.5) | collective-permute-done | bytes 1048608 | tf_op jit(solution)/shard_map/cond/branch_5_fun/ppermute | solution.py:143
  66.9 4.3 %shard_map.43 = bf16[512,1024]{1,0:T(8,128)(2,1)} custom-call(bf16[512,1024]{1,0:T(8,128)(2,1)} %get-tuple-element.153.raw_ref, f32[16,8,128]{2,1,0:T(8,128)} %get-tuple-element.154.totals_ref, bf16[1024,1024]{1,0:T(8,128)(2,1)S(1)} %get-tuple-element.155.centred_ref), custom_call_target="tpu_custom_call" | custom-call | flops 1073741824 | bytes 4194304 | tf_op jit(solution)/shard_map/pallas_call | solution.py:187
  71.2 0.0 copy-start.1
  71.2 6.4 %all-to-all-start.21 = ((bf16[8,64,1024]{2,1,0:T(8,128)(2,1)}), bf16[8,64,1024]{2,1,0:T(8,128)(2,1)S(1)}, u32[]{:S(2)}, u32[]{:S(2)}) async-start(bf16[8,64,1024]{2,1,0:T(8,128)(2,1)} %bitcast.9), calls=%async_computation.21 | async-start | bytes 2097152 | tf_op jit(solution)/shard_map/all_to_all | solution.py:201
  77.6 0.0 copy-done.1
  77.6 0.5 slice.15
  78.8 1.5 %convert_reduce_fusion = f32[128,1024]{1,0:T(8,128)S(1)} fusion(bf16[4,128,1024]{2,1,0:T(8,128)(2,1)} %get-tuple-element.158), kind=kLoop, calls=%fused_computation | loop fusion | flops 917504 | bytes 1572864 | tf_op jit(solution)/shard_map/reduce_sum | solution.py:197
  80.2 3.0 %collective-permute-start.15 = (bf16[64,1024]{1,0:T(8,128)(2,1)S(1)}, bf16[64,1024]{1,0:T(8,128)(2,1)S(1)}, u32[]{:S(2)}, u32[]{:S(2)}) collective-permute-start(bf16[64,1024]{1,0:T(8,128)(2,1)S(1)} %select_convert_fusion), channel_id=1, source_target_pairs={{0,8},{8,0},{1,9},{9,1},{2,10},{10,2},{3,11},{11,3},{4,12},{12,4},... | collective-permute-start | bytes 393224 | tf_op jit(solution)/shard_map/ppermute | solution.py:200
  83.3 11.5 %all-to-all-done.21.got_ref = bf16[8,64,1024]{2,1,0:T(8,128)(2,1)S(1)} async-done(((bf16[8,64,1024]{2,1,0:T(8,128)(2,1)}), bf16[8,64,1024]{2,1,0:T(8,128)(2,1)S(1)}, u32[]{:S(2)}, u32[]{:S(2)}) %all-to-all-start.21) | async-done | bytes 1048608 | tf_op jit(solution)/shard_map/all_to_all | solution.py:201
  94.9 1.0 shard_map.44
  95.9 12.6 %conditional.3 = (bf16[64,1024]{1,0:T(8,128)(2,1)}, bf16[16,32,128]{2,1,0:T(8,128)(2,1)}, s32[]{:T(128)}) conditional(s32[]{:T(128)} %bitcast.7, (bf16[64,1024]{1,0:T(8,128)(2,1)S(1)}, bf16[16,32,128]{2,1,0:T(8,128)(2,1)}) %shard_map.44, (bf16[64,1024]{1,0:T(8,128)(2,1)S(1)}, ...), branch_computations={%region_7.0_spmd, %region_8.9_spmd, %region_9.10_spmd, %region_10.... | conditional | flops 12 | bytes 917736 | solution.py:211
  95.9 0.0 collective-permute-start.12
  95.9 4.9 %all-to-all-start.19 = ((bf16[16,32,128]{2,1,0:T(8,128)(2,1)}), bf16[16,32,128]{2,1,0:T(8,128)(2,1)}, u32[]{:S(2)}, u32[]{:S(2)}) async-start(bf16[16,32,128]{2,1,0:T(8,128)(2,1)} %get-tuple-element.137), calls=%async_computation.19 | async-start | bytes 262144 | tf_op jit(solution)/shard_map/cond/branch_5_fun/all_to_all | solution.py:162
  100.8 7.8 %all-to-all-done.19 = bf16[16,32,128]{2,1,0:T(8,128)(2,1)} async-done(((bf16[16,32,128]{2,1,0:T(8,128)(2,1)}), bf16[16,32,128]{2,1,0:T(8,128)(2,1)}, u32[]{:S(2)}, u32[]{:S(2)}) %all-to-all-start.19) | async-done | bytes 131104 | tf_op jit(solution)/shard_map/cond/branch_5_fun/all_to_all | solution.py:162
  108.5 0.0 collective-permute-done.12
  108.5 0.0 collective-permute-done.15.other_ref
  108.5 1.9 %shard_map.45 = (f32[64,1024]{1,0:T(8,128)}, f32[2,64,1024]{2,1,0:T(8,128)}) custom-call(bf16[64,1024]{1,0:T(8,128)(2,1)} %get-tuple-element.156.arrived_ref, bf16[16,32,128]{2,1,0:T(8,128)(2,1)} %get-tuple-element.157.tiles_ref, f32[64,1024]{1,0:T(8,128)S(1)} %slice_select_fusion.keep_ref, bf16[64,1024]{1,0:T(8,128)(2,1)S(1)} %collective-permute-done.15.other_ref, ...), custom_call_target="tpu_custom_call" | custom-call | tf_op jit(solution)/shard_map/pallas_call | solution.py:215
  (2 shorter events, 0.1 us)
Async XLA Ops:
  0.6 4.0 %collective-permute-start.14 = (bf16[1024,512]{1,0:T(8,128)(2,1)}, bf16[1024,512]{1,0:T(8,128)(2,1)S(1)}, u32[]{:S(2)}, u32[]{:S(2)}) collective-permute-start(bf16[1024,512]{1,0:T(8,128)(2,1)} %own_ref.1), channel_id=1, source_target_pairs={{0,1},{1,0},{2,3},{3,2},{4,5},{5,4},{6,7},{7,6},{8,9},{9,8},{10,11... | collective-permute-start | bytes 3145736 | tf_op jit(solution)/shard_map/ppermute | solution.py:169
  1.4 0.7 copy-start
  2.1 3.4 %copy-start.2 = (bf16[1024,512]{1,0:T(8,128)(2,1)S(1)}, bf16[1024,512]{1,0:T(8,128)(2,1)}, u32[]{:S(2)}) copy-start(bf16[1024,512]{1,0:T(8,128)(2,1)} %own_ref.1) | copy-start | bytes 3145732
  5.5 15.9 %all-to-all-start.10 = ((f32[16,8,128]{2,1,0:T(8,128)}), f32[16,8,128]{2,1,0:T(8,128)S(1)}, u32[]{:S(2)}, u32[]{:S(2)}) async-start(f32[16,8,128]{2,1,0:T(8,128)} %get-tuple-element.117), calls=%async_computation.10 | async-start | bytes 131072 | tf_op jit(solution)/shard_map/cond/branch_5_fun/all_to_all | solution.py:135
  14.6 52.2 %collective-permute-start.5 = (bf16[512,1024]{1,0:T(8,128)(2,1)S(1)}, bf16[512,1024]{1,0:T(8,128)(2,1)}, u32[]{:S(2)}, u32[]{:S(2)}) collective-permute-start(bf16[512,1024]{1,0:T(8,128)(2,1)S(1)} %branch_5_fun.2), channel_id=1, source_target_pairs={{96,0},{112,16},{176,32},{160,48},{32,64},{48,80},{240,96},{224,11... | collective-permute-start | bytes 3145736 | tf_op jit(solution)/shard_map/cond/branch_5_fun/ppermute | solution.py:143
  21.4 2.5 %copy-start.8 = (f32[16,8,128]{2,1,0:T(8,128)}, f32[16,8,128]{2,1,0:T(8,128)S(1)}, u32[]{:S(2)}) copy-start(f32[16,8,128]{2,1,0:T(8,128)S(1)} %all-to-all-done.10.totals_ref) | copy-start | bytes 196612 | tf_op jit(solution)/shard_map/cond
  71.2 6.4 %copy-start.1 = (s32[2,16]{1,0:T(2,128)S(1)}, s32[2,16]{1,0:T(2,128)}, u32[]{:S(2)}) copy-start(s32[2,16]{1,0:T(2,128)} %partners_ref.1) | copy-start | bytes 388
  71.2 23.7 %all-to-all-start.21 = ((bf16[8,64,1024]{2,1,0:T(8,128)(2,1)}), bf16[8,64,1024]{2,1,0:T(8,128)(2,1)S(1)}, u32[]{:S(2)}, u32[]{:S(2)}) async-start(bf16[8,64,1024]{2,1,0:T(8,128)(2,1)} %bitcast.9), calls=%async_computation.21 | async-start | bytes 2097152 | tf_op jit(solution)/shard_map/all_to_all | solution.py:201
  80.2 28.3 %collective-permute-start.15 = (bf16[64,1024]{1,0:T(8,128)(2,1)S(1)}, bf16[64,1024]{1,0:T(8,128)(2,1)S(1)}, u32[]{:S(2)}, u32[]{:S(2)}) collective-permute-start(bf16[64,1024]{1,0:T(8,128)(2,1)S(1)} %select_convert_fusion), channel_id=1, source_target_pairs={{0,8},{8,0},{1,9},{9,1},{2,10},{10,2},{3,11},{11,3},{4,12},{12,4},... | collective-permute-start | bytes 393224 | tf_op jit(solution)/shard_map/ppermute | solution.py:200
  95.9 12.6 %collective-permute-start.12 = (bf16[64,1024]{1,0:T(8,128)(2,1)S(1)}, bf16[64,1024]{1,0:T(8,128)(2,1)}, u32[]{:S(2)}, u32[]{:S(2)}) collective-permute-start(bf16[64,1024]{1,0:T(8,128)(2,1)S(1)} %get-tuple-element.136), channel_id=1, source_target_pairs={{0,96},{16,112},{32,176},{48,160},{64,32},{80,48},{96,240},{112,22... | collective-permute-start | bytes 393224 | tf_op jit(solution)/shard_map/cond/branch_5_fun/ppermute | solution.py:161
  95.9 12.6 %all-to-all-start.19 = ((bf16[16,32,128]{2,1,0:T(8,128)(2,1)}), bf16[16,32,128]{2,1,0:T(8,128)(2,1)}, u32[]{:S(2)}, u32[]{:S(2)}) async-start(bf16[16,32,128]{2,1,0:T(8,128)(2,1)} %get-tuple-element.137), calls=%async_computation.19 | async-start | bytes 262144 | tf_op jit(solution)/shard_map/cond/branch_5_fun/all_to_all | solution.py:162
where the time goes:
time: 111 us; the launch traced here: 110 us
  waiting for transfers between devices  50.5 us (45%)
  starting transfers between devices  25.4 us (23%)
  blocking collectives  17.3 us (16%)
  Pallas kernels  12.6 us (11%)
  between operations  2 us (2%)
  other arithmetic  1.52 us (1%)
  local copies, waits for them, and re-layouts  1.21 us (1%)
    ppermute x1, waiting for transfers between devices, exchange(): lax.ppermute(half, SAMP, [(s, d) for d, s in enumerate(sources(mask))])  25.7 us
    all_to_all x1, blocking collectives, exchange(): diag = lax.all_to_all(partial.reshape(4, 128, 1024), 'x', 0, 0, tiled=True)  17.3 us
    all_to_all x1, waiting for transfers between devices, shards(): got = lax.all_to_all(partial.reshape(8, 64, 1024), CHIPS, 0, 0, tiled=True)  11.5 us
    all_to_all x1, starting transfers between devices, exchange(): totals = lax.all_to_all(total, SAMP, 0, 0, tiled=True)  9.04 us
    all_to_all x1, waiting for transfers between devices, finish(): turned = lax.all_to_all(tiles, PAR, 0, 0, tiled=True)  7.76 us
    all_to_all x1, starting transfers between devices, shards(): got = lax.all_to_all(partial.reshape(8, 64, 1024), CHIPS, 0, 0, tiled=True)  6.37 us
    all_to_all x1, waiting for transfers between devices, exchange(): totals = lax.all_to_all(total, SAMP, 0, 0, tiled=True)  5.48 us
    all_to_all x1, starting transfers between devices, finish(): turned = lax.all_to_all(tiles, PAR, 0, 0, tiled=True)  4.87 us
  transfers between devices with their start and end apart: 7, of which 4 were waited for; matrix products, arithmetic and copies ran while one was open for 2% of the time, Pallas kernels for 5%

commit v1 on v0

--- a/solution.py
+++ b/solution.py
@@ -156,11 +156,9 @@
     return raw, own, diag, totals
 
 
-def finish(mask, result, tiles):
+def finish(mask, result):
     back = [(d, s) for d, s in enumerate(sources(mask))]
-    arrived = lax.ppermute(result, SAMP, back)
-    turned = lax.all_to_all(tiles, PAR, 0, 0, tiled=True)
-    return arrived, turned, parity(lax.axis_index(SAMP), mask)
+    return lax.ppermute(result, SAMP, back), parity(lax.axis_index(SAMP), mask)
 
 
 def shards(jac, partners):
@@ -208,9 +206,8 @@
         [],
         1 << 20,
     )(got)
-    arrived, turned, par = lax.switch(
-        index, [functools.partial(finish, m) for m in range(1, 8)], result, tiles
-    )
+    turned = lax.all_to_all(tiles, PAR, 0, 0, tiled=True)
+    arrived, par = lax.switch(index, [functools.partial(finish, m) for m in range(1, 8)], result)
     place = par ^ (first > 7).astype(jnp.int32)
     return pl.pallas_call(
         output_kernel,

time: 111 us -> 86.2 us (0.78)
  waiting for transfers between devices: 50.5 us -> 27.6 us
  starting transfers between devices: 25.4 us -> 23.7 us
    ppermute x1, waiting for transfers between devices: 25.7 us -> 2.01 us  [exchange(): lax.ppermute(half, SAMP, [(s, d) for d, s in enumerate(sources(mask))])]
    all_to_all x1, waiting for transfers between devices: 7.76 us -> 2.55 us  [shards(): turned = lax.all_to_all(tiles, PAR, 0, 0, tiled=True)]
    ppermute x1, waiting for transfers between devices: 0.01 us -> 4.95 us  [finish(): lax.ppermute(result, SAMP, back)]
  transfers between devices with their start and end apart: 7 -> 7, of which waited for: 4 -> 5; matrix products, arithmetic and copies ran while one was open for 2% -> 2% of each run, Pallas kernels for 5% -> 6%
where the time goes in v1:
time: 86.2 us; the launch traced here: 85.8 us
  waiting for transfers between devices  27.6 us (32%)
  starting transfers between devices  23.7 us (27%)
  blocking collectives  17.3 us (20%)
  Pallas kernels  12.5 us (15%)
  between operations  2 us (2%)
  other arithmetic  1.52 us (2%)
  local copies, waits for them, and re-layouts  1.21 us (1%)
    all_to_all x1, blocking collectives, exchange(): diag = lax.all_to_all(partial.reshape(4, 128, 1024), 'x', 0, 0, tiled=True)  17.3 us
    all_to_all x1, waiting for transfers between devices, shards(): got = lax.all_to_all(partial.reshape(8, 64, 1024), CHIPS, 0, 0, tiled=True)  11.6 us
    all_to_all x1, starting transfers between devices, exchange(): totals = lax.all_to_all(total, SAMP, 0, 0, tiled=True)  9.04 us
    all_to_all x1, waiting for transfers between devices, exchange(): totals = lax.all_to_all(total, SAMP, 0, 0, tiled=True)  6.51 us
    all_to_all x1, starting transfers between devices, shards(): got = lax.all_to_all(partial.reshape(8, 64, 1024), CHIPS, 0, 0, tiled=True)  6.37 us
    ppermute x1, waiting for transfers between devices, finish(): lax.ppermute(result, SAMP, back)  4.95 us
    pallas_call x1, Pallas kernels, shards(): pl.pallas_call(cross_kernel, out_shape=jax.ShapeDtypeStruct((512, 1024),...  4.28 us
    all_to_all x1, starting transfers between devices, shards(): turned = lax.all_to_all(tiles, PAR, 0, 0, tiled=True)  4.16 us
  transfers between devices with their start and end apart: 7, of which 5 were waited for; matrix products, arithmetic and copies ran while one was open for 2% of the time, Pallas kernels for 6%

profile of v1, /device:TPU:33, one launch (start us, length us, event | category | flops | bytes accessed | tf_op | source)
XLA Modules:
  0.0 85.8 jit_solution(13144601281031249077)
XLA Ops:
  0.6 0.8 collective-permute-start.14
  1.4 0.0 copy-start
  1.4 0.7 copy-done
  2.1 0.0 copy-start.2
  2.1 1.9 %shard_map.41 = (f32[16,8,128]{2,1,0:T(8,128)S(1)}, s32[1]{0:T(128)}) custom-call(bf16[1024,512]{1,0:T(8,128)(2,1)} %own_ref.1, s32[2,16]{1,0:T(2,128)S(1)} %copy-done), custom_call_target="tpu_custom_call" | custom-call | flops 16777216 | bytes 1048576 | tf_op jit(solution)/shard_map/pallas_call | solution.py:169
  4.6 0.0 collective-permute-done.14.sister_ref
  4.6 0.9 %shard_map.42 = f32[16,8,128]{2,1,0:T(8,128)} custom-call(bf16[1024,512]{1,0:T(8,128)(2,1)S(1)} %collective-permute-done.14.sister_ref, f32[16,8,128]{2,1,0:T(8,128)S(1)} %get-tuple-element.118.before_ref), custom_call_target="tpu_custom_call" | custom-call | flops 16777216 | bytes 6291456 | tf_op jit(solution)/shard_map/pallas_call | solution.py:178
  5.5 0.0 copy-done.2
  5.5 37.6 %conditional.2 = (bf16[512,1024]{1,0:T(8,128)(2,1)}, bf16[1024,1024]{1,0:T(8,128)(2,1)S(1)}, bf16[4,128,1024]{2,1,0:T(8,128)(2,1)}, f32[16,8,128]{2,1,0:T(8,128)}) conditional(s32[]{:T(128)} %bitcast.7, (bf16[1024,512]{1,0:T(8,128)(2,1)S(1)}, bf16[1024,512]{1,0:T(8,128)(2,1)S(1)}, s32[1]{0:T(128)}, ...), branch_computations={%region_0.0_spmd, %region_1.0_spmd, %region_2.0_spmd, %region_3.0_... | conditional | flops 4294967296 | bytes 15138948 | solution.py:179
  5.5 9.0 %all-to-all-start.2 = ((f32[16,8,128]{2,1,0:T(8,128)}), f32[16,8,128]{2,1,0:T(8,128)S(1)}, u32[]{:S(2)}, u32[]{:S(2)}) async-start(f32[16,8,128]{2,1,0:T(8,128)} %get-tuple-element.72), calls=%async_computation.2 | async-start | bytes 131072 | tf_op jit(solution)/shard_map/cond/branch_1_fun/all_to_all | solution.py:135
  14.5 0.1 branch_1_fun.2
  14.6 0.2 collective-permute-start.1
  14.8 6.5 %all-to-all-done.2.totals_ref = f32[16,8,128]{2,1,0:T(8,128)S(1)} async-done(((f32[16,8,128]{2,1,0:T(8,128)}), f32[16,8,128]{2,1,0:T(8,128)S(1)}, u32[]{:S(2)}, u32[]{:S(2)}) %all-to-all-start.2) | async-done | bytes 65568 | tf_op jit(solution)/shard_map/cond/branch_1_fun/all_to_all | solution.py:135
  21.3 0.0 copy-start.4
  21.3 2.5 %branch_1_fun.3 = (bf16[1024,1024]{1,0:T(8,128)(2,1)S(1)}, bf16[512,1024]{1,0:T(8,128)(2,1)S(1)}) custom-call(bf16[1024,512]{1,0:T(8,128)(2,1)S(1)} %get-tuple-element.69.own_ref, bf16[1024,512]{1,0:T(8,128)(2,1)S(1)} %get-tuple-element.70.sister_ref, f32[16,8,128]{2,1,0:T(8,128)S(1)} %all-to-all-done.2.totals_ref, s32[1]{0:T(128)} %get-tuple-element.71.core_ref), custom_call_target="tpu_custom_call" | custom-call | flops 4294967296 | bytes 6291456 | tf_op jit(solution)/shard_map/cond/branch_1_fun/pallas_call | solution.py:144
  23.8 0.0 copy-done.4
  23.8 17.3 %all_to_all.67 = bf16[4,128,1024]{2,1,0:T(8,128)(2,1)} all-to-all(bf16[4,128,1024]{2,1,0:T(8,128)(2,1)S(1)} %bitcast.13), channel_id=1, replica_groups=mesh['z'=8,'y_lo'=2,'y_hi'=2,'x'=4,'core'=2] {'x'}, dimensions={0} | all-to-all | bytes 2097152 | tf_op jit(solution)/shard_map/cond/branch_1_fun/all_to_all | solution.py:155
  41.1 2.0 %collective-permute-done.1 = bf16[512,1024]{1,0:T(8,128)(2,1)} collective-permute-done((bf16[512,1024]{1,0:T(8,128)(2,1)S(1)}, bf16[512,1024]{1,0:T(8,128)(2,1)}, u32[]{:S(2)}, u32[]{:S(2)}) %collective-permute-start.1) | collective-permute-done | bytes 1048608 | tf_op jit(solution)/shard_map/cond/branch_1_fun/ppermute | solution.py:143
  43.1 4.3 %shard_map.43 = bf16[512,1024]{1,0:T(8,128)(2,1)} custom-call(bf16[512,1024]{1,0:T(8,128)(2,1)} %get-tuple-element.119.raw_ref, f32[16,8,128]{2,1,0:T(8,128)} %get-tuple-element.120.totals_ref, bf16[1024,1024]{1,0:T(8,128)(2,1)S(1)} %get-tuple-element.121.centred_ref), custom_call_target="tpu_custom_call" | custom-call | flops 1073741824 | bytes 4194304 | tf_op jit(solution)/shard_map/pallas_call | solution.py:185
  47.4 0.0 copy-start.1
  47.4 6.4 %all-to-all-start.14 = ((bf16[8,64,1024]{2,1,0:T(8,128)(2,1)}), bf16[8,64,1024]{2,1,0:T(8,128)(2,1)S(1)}, u32[]{:S(2)}, u32[]{:S(2)}) async-start(bf16[8,64,1024]{2,1,0:T(8,128)(2,1)} %bitcast.9), calls=%async_computation.14 | async-start | bytes 2097152 | tf_op jit(solution)/shard_map/all_to_all | solution.py:199
  53.8 0.0 copy-done.1
  53.8 0.5 slice.15
  55.0 1.5 %convert_reduce_fusion = f32[128,1024]{1,0:T(8,128)S(1)} fusion(bf16[4,128,1024]{2,1,0:T(8,128)(2,1)} %get-tuple-element.125), kind=kLoop, calls=%fused_computation | loop fusion | flops 917504 | bytes 1572864 | tf_op jit(solution)/shard_map/reduce_sum | solution.py:195
  56.5 3.0 %collective-permute-start.15 = (bf16[64,1024]{1,0:T(8,128)(2,1)S(1)}, bf16[64,1024]{1,0:T(8,128)(2,1)S(1)}, u32[]{:S(2)}, u32[]{:S(2)}) collective-permute-start(bf16[64,1024]{1,0:T(8,128)(2,1)S(1)} %select_convert_fusion), channel_id=1, source_target_pairs={{0,8},{8,0},{1,9},{9,1},{2,10},{10,2},{3,11},{11,3},{4,12},{12,4},... | collective-permute-start | bytes 393224 | tf_op jit(solution)/shard_map/ppermute | solution.py:198
  59.5 11.6 %all-to-all-done.14.got_ref = bf16[8,64,1024]{2,1,0:T(8,128)(2,1)S(1)} async-done(((bf16[8,64,1024]{2,1,0:T(8,128)(2,1)}), bf16[8,64,1024]{2,1,0:T(8,128)(2,1)S(1)}, u32[]{:S(2)}, u32[]{:S(2)}) %all-to-all-start.14) | async-done | bytes 1048608 | tf_op jit(solution)/shard_map/all_to_all | solution.py:199
  71.1 1.0 %shard_map.44 = (bf16[64,1024]{1,0:T(8,128)(2,1)S(1)}, bf16[16,32,128]{2,1,0:T(8,128)(2,1)}) custom-call(bf16[8,64,1024]{2,1,0:T(8,128)(2,1)S(1)} %all-to-all-done.14.got_ref), custom_call_target="tpu_custom_call" | custom-call | flops 1048576 | bytes 6291456 | tf_op jit(solution)/shard_map/pallas_call | solution.py:200
  72.1 4.2 %all-to-all-start.15 = ((bf16[16,32,128]{2,1,0:T(8,128)(2,1)}), bf16[16,32,128]{2,1,0:T(8,128)(2,1)S(1)}, u32[]{:S(2)}, u32[]{:S(2)}) async-start(bf16[16,32,128]{2,1,0:T(8,128)(2,1)} %get-tuple-element.124), calls=%async_computation.15 | async-start | bytes 262144 | tf_op jit(solution)/shard_map/all_to_all | solution.py:209
  76.3 5.1 %conditional.3 = (bf16[64,1024]{1,0:T(8,128)(2,1)}, s32[]{:T(128)}) conditional(s32[]{:T(128)} %bitcast.7, bf16[64,1024]{1,0:T(8,128)(2,1)S(1)} %get-tuple-element.122, bf16[64,1024]{1,0:T(8,128)(2,1)S(1)} %get-tuple-element.122, bf16[64,1024]{1,0:T(8,128)(2,1)S(1)} %get-tuple-element.122, ...), branch_computations={%region_7.0_spmd, %region_8.9_spmd, %region_9.10_spmd, %region_10.... | conditional | flops 12 | bytes 524480 | solution.py:210
  76.3 0.1 collective-permute-start.8
  76.4 5.0 %collective-permute-done.8 = bf16[64,1024]{1,0:T(8,128)(2,1)} collective-permute-done((bf16[64,1024]{1,0:T(8,128)(2,1)S(1)}, bf16[64,1024]{1,0:T(8,128)(2,1)}, u32[]{:S(2)}, u32[]{:S(2)}) %collective-permute-start.8) | collective-permute-done | bytes 131104 | tf_op jit(solution)/shard_map/cond/branch_1_fun/ppermute | solution.py:161
  81.4 0.0 collective-permute-done.15.other_ref
  81.4 2.5 %all-to-all-done.15.tiles_ref = bf16[16,32,128]{2,1,0:T(8,128)(2,1)S(1)} async-done(((bf16[16,32,128]{2,1,0:T(8,128)(2,1)}), bf16[16,32,128]{2,1,0:T(8,128)(2,1)S(1)}, u32[]{:S(2)}, u32[]{:S(2)}) %all-to-all-start.15) | async-done | bytes 131104 | tf_op jit(solution)/shard_map/all_to_all | solution.py:209
  83.9 1.8 %shard_map.45 = (f32[64,1024]{1,0:T(8,128)}, f32[2,64,1024]{2,1,0:T(8,128)}) custom-call(bf16[64,1024]{1,0:T(8,128)(2,1)} %get-tuple-element.123.arrived_ref, bf16[16,32,128]{2,1,0:T(8,128)(2,1)S(1)} %all-to-all-done.15.tiles_ref, f32[64,1024]{1,0:T(8,128)S(1)} %slice_select_fusion.keep_ref, bf16[64,1024]{1,0:T(8,128)(2,1)S(1)} %collective-permute-done.15.other_ref, ...), custom_call_target="tpu_custom_call" | custom-call | tf_op jit(solution)/shard_map/pallas_call | solution.py:212
  (2 shorter events, 0.1 us)
Async XLA Ops:
  0.6 4.0 %collective-permute-start.14 = (bf16[1024,512]{1,0:T(8,128)(2,1)}, bf16[1024,512]{1,0:T(8,128)(2,1)S(1)}, u32[]{:S(2)}, u32[]{:S(2)}) collective-permute-start(bf16[1024,512]{1,0:T(8,128)(2,1)} %own_ref.1), channel_id=1, source_target_pairs={{0,1},{1,0},{2,3},{3,2},{4,5},{5,4},{6,7},{7,6},{8,9},{9,8},{10,11... | collective-permute-start | bytes 3145736 | tf_op jit(solution)/shard_map/ppermute | solution.py:167
  1.4 0.7 copy-start
  2.1 3.4 %copy-start.2 = (bf16[1024,512]{1,0:T(8,128)(2,1)S(1)}, bf16[1024,512]{1,0:T(8,128)(2,1)}, u32[]{:S(2)}) copy-start(bf16[1024,512]{1,0:T(8,128)(2,1)} %own_ref.1) | copy-start | bytes 3145732
  5.5 15.8 %all-to-all-start.2 = ((f32[16,8,128]{2,1,0:T(8,128)}), f32[16,8,128]{2,1,0:T(8,128)S(1)}, u32[]{:S(2)}, u32[]{:S(2)}) async-start(f32[16,8,128]{2,1,0:T(8,128)} %get-tuple-element.72), calls=%async_computation.2 | async-start | bytes 131072 | tf_op jit(solution)/shard_map/cond/branch_1_fun/all_to_all | solution.py:135
  14.6 28.5 %collective-permute-start.1 = (bf16[512,1024]{1,0:T(8,128)(2,1)S(1)}, bf16[512,1024]{1,0:T(8,128)(2,1)}, u32[]{:S(2)}, u32[]{:S(2)}) collective-permute-start(bf16[512,1024]{1,0:T(8,128)(2,1)S(1)} %branch_1_fun.2), channel_id=1, source_target_pairs={{32,0},{48,16},{240,32},{224,48},{96,64},{112,80},{176,96},{160,11... | collective-permute-start | bytes 3145736 | tf_op jit(solution)/shard_map/cond/branch_1_fun/ppermute | solution.py:143
  21.3 2.5 %copy-start.4 = (f32[16,8,128]{2,1,0:T(8,128)}, f32[16,8,128]{2,1,0:T(8,128)S(1)}, u32[]{:S(2)}) copy-start(f32[16,8,128]{2,1,0:T(8,128)S(1)} %all-to-all-done.2.totals_ref) | copy-start | bytes 196612 | tf_op jit(solution)/shard_map/cond
  47.4 6.4 %copy-start.1 = (s32[2,16]{1,0:T(2,128)S(1)}, s32[2,16]{1,0:T(2,128)}, u32[]{:S(2)}) copy-start(s32[2,16]{1,0:T(2,128)} %partners_ref.1) | copy-start | bytes 388
  47.4 23.7 %all-to-all-start.14 = ((bf16[8,64,1024]{2,1,0:T(8,128)(2,1)}), bf16[8,64,1024]{2,1,0:T(8,128)(2,1)S(1)}, u32[]{:S(2)}, u32[]{:S(2)}) async-start(bf16[8,64,1024]{2,1,0:T(8,128)(2,1)} %bitcast.9), calls=%async_computation.14 | async-start | bytes 2097152 | tf_op jit(solution)/shard_map/all_to_all | solution.py:199
  56.5 24.9 %collective-permute-start.15 = (bf16[64,1024]{1,0:T(8,128)(2,1)S(1)}, bf16[64,1024]{1,0:T(8,128)(2,1)S(1)}, u32[]{:S(2)}, u32[]{:S(2)}) collective-permute-start(bf16[64,1024]{1,0:T(8,128)(2,1)S(1)} %select_convert_fusion), channel_id=1, source_target_pairs={{0,8},{8,0},{1,9},{9,1},{2,10},{10,2},{3,11},{11,3},{4,12},{12,4},... | collective-permute-start | bytes 393224 | tf_op jit(solution)/shard_map/ppermute | solution.py:198
  72.1 11.8 %all-to-all-start.15 = ((bf16[16,32,128]{2,1,0:T(8,128)(2,1)}), bf16[16,32,128]{2,1,0:T(8,128)(2,1)S(1)}, u32[]{:S(2)}, u32[]{:S(2)}) async-start(bf16[16,32,128]{2,1,0:T(8,128)(2,1)} %get-tuple-element.124), calls=%async_computation.15 | async-start | bytes 262144 | tf_op jit(solution)/shard_map/all_to_all | solution.py:209
  76.3 5.1 %collective-permute-start.8 = (bf16[64,1024]{1,0:T(8,128)(2,1)S(1)}, bf16[64,1024]{1,0:T(8,128)(2,1)}, u32[]{:S(2)}, u32[]{:S(2)}) collective-permute-start(bf16[64,1024]{1,0:T(8,128)(2,1)S(1)} %param.8), channel_id=1, source_target_pairs={{0,32},{16,48},{32,240},{48,224},{64,96},{80,112},{96,176},{112,16... | collective-permute-start | bytes 393224 | tf_op jit(solution)/shard_map/cond/branch_1_fun/ppermute | solution.py:161
